TPU v7x, 32 devices: a whole 2x2x4 slice. The times are simulated.
32 devices in a mesh: row: 8 (over y, x, core), col: 4 (over z).
Axes of the slice: x: 2, y: 2, z: 4, core: 2. Of those that a mesh axis runs over, the one named last changes fastest.
Arguments:
- right_sides: float32 [15, 512, 4096], P(None, 'row', 'col'), may hold values from -6 to 6
- diag_inverse: bfloat16 [15, 4096, 4096], P(None, 'row', 'col'), may hold values from -2 to 2, as said below
- panels: bfloat16 [14, 3, 4096, 4096], P(None, None, 'col', 'row'), may hold values from -0.046875 to 0.046875
- block_map: int32 [14, 4, 3], replicated, may hold values from 8 to 15, as said below
Outputs:
- solution: float32 [15, 512, 4096], P(None, 'col', 'row')
Inputs may be any that keep to these rules, and one draw needn't show every extreme that they name: `block_map`: entry [s, q, c] is an ancestor of supernode s, or 15, which marks an empty slot; the ancestors named in one [s, q] are distinct. Each diag_inverse[n] is lower triangular: entries whose column index exceeds the row index are zero.
All inputs are finite; a program needn't handle non-finite values.
Results may differ from a plain program's by a relative error of at most 0.028.
Values may be sent and summed in bfloat16 or wider, within the bound.
A program may use at most 192 MiB of HBM per device.

v0:
```python
import jax
import jax.numpy as jnp
from jax import lax
from jax.sharding import PartitionSpec as P

LEV = 4
S = 15


def per_device(right_sides, diag_inverse, panels, block_map):
    col_index = lax.axis_index("col")
    share_cols = right_sides.shape[2]
    samples = right_sides.shape[1] * lax.axis_size("row")
    first_target = 2 ** (LEV - 1)
    pending = jnp.zeros((samples, S - first_target, share_cols), jnp.float32)
    own_blocks = lax.dynamic_slice_in_dim(block_map, col_index, 1, 1)[:, 0, :]
    results = []
    for level_index in range(LEV - 1, -1, -1):
        first_node = 2**LEV - 2 ** (level_index + 1)
        node_count = 2**level_index
        pending_first = first_node - first_target
        current = right_sides[first_node : first_node + node_count]
        if level_index < LEV - 1:
            summed_update = lax.psum_scatter(
                pending[:, pending_first : pending_first + node_count].astype(jnp.bfloat16),
                "row",
                scatter_dimension=0,
                tiled=True,
            ).astype(jnp.float32)
            current = current - jnp.swapaxes(summed_update, 0, 1)
        gathered = lax.all_gather(current.astype(jnp.bfloat16), "row", axis=1, tiled=True)
        inverse = diag_inverse[first_node : first_node + node_count]
        own_rows = lax.psum_scatter(
            jnp.einsum(
                "nck,nik->cni", gathered, inverse, preferred_element_type=jnp.float32
            ).astype(jnp.bfloat16),
            "col",
            scatter_dimension=0,
            tiled=True,
        ).astype(jnp.float32)
        if level_index > 0:
            solved_all = lax.all_gather(own_rows.astype(jnp.bfloat16), "col", axis=0, tiled=True)
        results.append(jnp.swapaxes(own_rows, 0, 1))
        if level_index > 0:
            node_panels = panels[first_node : first_node + node_count]
            node_maps = own_blocks[first_node : first_node + node_count]
            products = jnp.einsum(
                "cnk,nsik->nsci", solved_all, node_panels, preferred_element_type=jnp.float32
            )
            selector = (
                node_maps[:, :, None] == first_target + jnp.arange(S - first_target)[None, None, :]
            ).astype(jnp.float32)
            pending = pending + jnp.einsum(
                "nst,nsci->cti", selector, products, precision=lax.Precision.HIGHEST
            )
    return jnp.concatenate(results, axis=0)


def solution(mesh):
    return jax.shard_map(
        per_device,
        mesh=mesh,
        in_specs=(P(None, "row", "col"), P(None, "row", "col"), P(None, None, "col", "row"), P()),
        out_specs=P(None, "col", "row"),
        check_vma=False,
    )
```

profile of v0, /device:TPU:0, one launch (start us, length us, event | category | flops | bytes accessed | tf_op | source)
XLA Modules:
  0.0 1013.3 jit_solution(4509241968812859626)
XLA Ops:
  6.5 2.7 slice.106
  9.3 57.2 %all-gather.8.cloned.1.call-done = bf16[8,512,1024]{2,1,0:T(8,128)(2,1)} async-done(((bf16[8,64,1024]{2,1,0:T(8,128)(2,1)}), bf16[8,512,1024]{2,1,0:T(8,128)(2,1)}) %all-gather.8.cloned.1.call-update) | async-done | bytes 8388624 | tf_op jit(solution)/shard_map/all_gather | solution.py:31
  66.5 12.3 %convolution_convert_fusion = bf16[8,512,512]{2,1,0:T(8,128)(2,1)} fusion(bf16[15,512,1024]{2,1,0:T(8,128)(2,1)} %param.5, bf16[8,512,1024]{2,1,0:T(8,128)(2,1)} %all-gather.8.cloned.1.call-done), kind=kOutput, calls=%fused_computation.26 | convolution fusion | flops 4297064448 | bytes 28311552 | tf_op jit(solution)/shard_map/nck,nik->cni/dot_general | solution.py:34
  78.8 6.4 copy.63
  85.3 76.9 %reduce-scatter.13.cloned.1.call-done = bf16[128,4096]{1,0:T(8,128)(2,1)} async-done(((bf16[512,4096]{1,0:T(8,128)(2,1)}), bf16[128,4096]{1,0:T(8,128)(2,1)}) %reduce-scatter.13.cloned.1.call-update) | async-done | bytes 1048592
  162.1 1.6 copy.64
  163.8 1.3 copy.30
  165.1 0.3 all-reduce.7.cloned.1.call-start
  165.5 81.0 %all-gather.10.cloned.1.call-done = bf16[512,8,512]{2,0,1:T(8,128)(2,1)} async-done(((bf16[128,8,512]{2,0,1:T(8,128)(2,1)}), bf16[512,8,512]{2,0,1:T(8,128)(2,1)}) %all-gather.10.cloned.1.call-update) | async-done | bytes 4194320 | tf_op jit(solution)/shard_map/all_gather | solution.py:42
  246.5 29.1 %fusion.6 = f32[8,3,512,1024]{3,2,1,0:T(8,128)} fusion(bf16[14,3,1024,512]{3,2,1,0:T(8,128)(2,1)} %param.6, bf16[512,8,512]{2,0,1:T(8,128)(2,1)} %all-gather.10.cloned.1.call-done), kind=kOutput, calls=%fused_computation.6 | convolution fusion | flops 12884901888 | bytes 79691776 | tf_op jit(solution)/shard_map/cnk,nsik->nsci/dot_general | solution.py:47
  275.7 86.6 %fusion = f32[512,1024,7,1]{1,2,3,0:T(8,128)} fusion(f32[8,3,512,1024]{3,2,1,0:T(8,128)} %fusion.6, s32[8,3]{0,1:T(4,128)S(1)} %bitcast.120, s32[7]{0:T(128)S(1)} %iota_add_fusion), kind=kOutput, calls=%fused_computation | convolution fusion | flops 1056964736 | bytes 65011836 | tf_op jit(solution)/shard_map/nst,nsci->cti/dot_general | solution.py:53
  362.3 7.2 fusion.19
  369.5 4.0 slice.76
  373.6 0.6 dynamic-slice
  374.8 78.4 %all-reduce.7.cloned.1.call-done = bf16[512,4,1024]{2,1,0:T(4,128)(2,1)} async-done(((bf16[512,4,1024]{2,1,0:T(4,128)(2,1)}), bf16[512,4,1024]{2,1,0:T(4,128)(2,1)}) %all-reduce.7.cloned.1.call-update) | async-done | bytes 4194320
  453.2 2.6 fusion.50
  456.0 36.9 %all-gather.12.cloned.1.call-done = bf16[4,512,1024]{2,0,1:T(4,128)(2,1)} async-done(((bf16[4,64,1024]{2,0,1:T(4,128)(2,1)}), bf16[4,512,1024]{2,0,1:T(4,128)(2,1)}) %all-gather.12.cloned.1.call-update) | async-done | bytes 4194320 | tf_op jit(solution)/shard_map/all_gather | solution.py:31
  492.9 6.4 convert_bitcast_fusion.1
  499.2 1.6 copy.75
  500.9 44.0 %reduce-scatter.15.cloned.1.call-done = bf16[128,2048]{1,0:T(8,128)(2,1)} async-done(((bf16[512,2048]{1,0:T(8,128)(2,1)}), bf16[128,2048]{1,0:T(8,128)(2,1)}) %reduce-scatter.15.cloned.1.call-update) | async-done | bytes 524304
  544.9 1.3 copy.66
  546.2 1.0 copy.35
  547.4 45.3 %all-gather.14.cloned.1.call-done = bf16[512,4,512]{2,0,1:T(8,128)(2,1)} async-done(((bf16[128,4,512]{2,0,1:T(8,128)(2,1)}), bf16[512,4,512]{2,0,1:T(8,128)(2,1)}) %all-gather.14.cloned.1.call-update) | async-done | bytes 2097168 | tf_op jit(solution)/shard_map/all_gather | solution.py:42
  592.7 15.3 %fusion.16 = f32[4,3,512,1024]{3,2,1,0:T(8,128)} fusion(bf16[14,3,1024,512]{3,2,1,0:T(8,128)(2,1)} %param.6, bf16[512,4,512]{2,0,1:T(8,128)(2,1)} %all-gather.14.cloned.1.call-done), kind=kOutput, calls=%fused_computation.15 | convolution fusion | flops 6442450944 | bytes 39845888 | tf_op jit(solution)/shard_map/cnk,nsik->nsci/dot_general | solution.py:47
  608.0 60.1 %bitcast_add_fusion.1 = f32[512,1024,7]{1,2,0:T(8,128)} fusion(f32[512,1024,7,1]{1,2,3,0:T(8,128)} %fusion, f32[4,3,512,1024]{3,2,1,0:T(8,128)} %fusion.16, s32[7]{0:T(128)S(1)} %iota_add_fusion, s32[4,3]{0,1:T(4,128)S(1)} %bitcast.121), kind=kOutput, calls=%fused_computation.9 | convolution fusion | flops 532152384 | bytes 54526028 | tf_op jit(solution)/shard_map/nst,nsci->cti/dot_general | solution.py:53
  668.0 6.6 convert_bitcast_fusion
  674.7 3.7 slice.77
  678.5 60.3 %all-reduce.9.cloned.1.call-done = bf16[512,2,1024]{2,1,0:T(2,128)(2,1)} async-done(((bf16[512,2,1024]{2,1,0:T(2,128)(2,1)}), bf16[512,2,1024]{2,1,0:T(2,128)(2,1)}) %all-reduce.9.cloned.1.call-update) | async-done | bytes 2097168
  738.8 2.2 fusion.55
  741.1 27.2 %all-gather.16.cloned.1.call-done = bf16[2,512,1024]{2,0,1:T(2,128)(2,1)} async-done(((bf16[2,64,1024]{2,0,1:T(2,128)(2,1)}), bf16[2,512,1024]{2,0,1:T(2,128)(2,1)}) %all-gather.16.cloned.1.call-update) | async-done | bytes 2097168 | tf_op jit(solution)/shard_map/all_gather | solution.py:31
  768.3 3.5 fusion.45
  771.8 1.1 copy.76
  773.0 27.2 %reduce-scatter.17.cloned.1.call-done = bf16[128,1024]{1,0:T(8,128)(2,1)} async-done(((bf16[512,1024]{1,0:T(8,128)(2,1)}), bf16[128,1024]{1,0:T(8,128)(2,1)}) %reduce-scatter.17.cloned.1.call-update) | async-done | bytes 262160
  800.2 1.1 copy.68
  801.3 0.9 copy.42
  802.5 26.5 %all-gather.18.cloned.1.call-done = bf16[512,2,512]{2,0,1:T(8,128)(2,1)} async-done(((bf16[128,2,512]{2,0,1:T(8,128)(2,1)}), bf16[512,2,512]{2,0,1:T(8,128)(2,1)}) %all-gather.18.cloned.1.call-update) | async-done | bytes 1048592 | tf_op jit(solution)/shard_map/all_gather | solution.py:42
  829.0 11.1 %fusion.25 = f32[2,3,512,1024]{3,2,1,0:T(8,128)} fusion(bf16[14,3,1024,512]{3,2,1,0:T(8,128)(2,1)} %param.6, bf16[512,2,512]{2,0,1:T(8,128)(2,1)} %all-gather.18.cloned.1.call-done), kind=kOutput, calls=%fused_computation.21 | convolution fusion | flops 3221225472 | bytes 19922944 | tf_op jit(solution)/shard_map/cnk,nsik->nsci/dot_general | solution.py:47
  840.1 39.9 %fusion.20 = bf16[512,7,1024]{2,1,0:T(8,128)(2,1)} fusion(f32[512,1024,7]{1,2,0:T(8,128)} %bitcast_add_fusion.1, f32[2,3,512,1024]{3,2,1,0:T(8,128)} %fusion.25, s32[7]{0:T(128)S(1)} %iota_add_fusion, s32[2,3]{1,0:T(2,128)S(1)} %bitcast.122), kind=kOutput, calls=%fused_computation.17 | convolution fusion | flops 271581216 | bytes 34603060 | tf_op jit(solution)/shard_map/nst,nsci->cti/dot_general | solution.py:53
  880.0 7.0 slice.78
  887.1 61.0 %all-reduce.11.cloned.1.call-done = bf16[512,1,1024]{2,1,0:T(2,128)(2,1)} async-done(((bf16[512,1,1024]{2,1,0:T(2,128)(2,1)}), bf16[512,1,1024]{2,1,0:T(2,128)(2,1)}) %all-reduce.11.cloned.1.call-update) | async-done | bytes 1048592
  948.1 1.4 fusion.56
  949.5 0.7 copy.45
  950.3 22.8 %all-gather.20.cloned.1.call-done = bf16[1,512,1024]{2,1,0:T(8,128)(2,1)} async-done(((bf16[1,64,1024]{2,1,0:T(8,128)(2,1)}), bf16[1,512,1024]{2,1,0:T(8,128)(2,1)}) %all-gather.20.cloned.1.call-update) | async-done | bytes 1048592 | tf_op jit(solution)/shard_map/all_gather | solution.py:31
  973.1 3.1 convolution_convert_fusion.1
  976.2 21.7 %reduce-scatter.19.cloned.1.call-done = bf16[128,512]{1,0:T(8,128)(2,1)} async-done(((bf16[512,512]{1,0:T(8,128)(2,1)}), bf16[128,512]{1,0:T(8,128)(2,1)}) %reduce-scatter.19.cloned.1.call-update) | async-done | bytes 131088
  997.9 1.0 copy.70
  998.9 2.2 maximum_convert_fusion
  1001.2 5.4 copy.47
  (44 shorter events, 1.0 us)
Async XLA Ops:
  6.5 158.9 %copy-start = (s32[14,4,3]{0,1,2:T(4,128)S(1)}, s32[14,4,3]{0,1,2:T(4,128)}, u32[]{:S(2)}) copy-start(s32[14,4,3]{0,1,2:T(4,128)} %param.7) | copy-start | bytes 2020
  6.5 60.0 %all-gather.8.cloned.1.call-start = ((), (), s32[]{:S(2)}) async-start(), calls=%async_computation.4 | async-start | bytes 9437184 | tf_op jit(solution)/shard_map/all_gather | solution.py:31
  9.3 152.8 %reduce-scatter.13.cloned.1.call-start = ((), (), s32[]{:S(2)}) async-start(), calls=%async_computation.11 | async-start | bytes 5242880
  85.2 161.3 %all-gather.10.cloned.1.call-start = ((), (), s32[]{:S(2)}) async-start(), calls=%async_computation.5 | async-start | bytes 5242880 | tf_op jit(solution)/shard_map/all_gather | solution.py:42
  165.1 288.1 %all-reduce.7.cloned.1.call-start = ((), (), s32[]{:S(2)}) async-start(), calls=%async_computation.15 | async-start | bytes 8388608
  369.5 4.1 copy-start.1
  369.5 83.8 %slice-start = ((f32[15,64,1024]{2,1,0:T(8,128)}), f32[4,64,1024]{2,1,0:T(8,128)S(1)}, s32[]{:S(2)}) async-start(f32[15,64,1024]{2,1,0:T(8,128)} %param.4), calls=%async_computation.18 | async-start | bytes 2097152 | tf_op jit(solution)/shard_map/slice | solution.py:22
  373.5 119.3 %all-gather.12.cloned.1.call-start = ((), (), s32[]{:S(2)}) async-start(), calls=%async_computation.6 | async-start | bytes 4718592 | tf_op jit(solution)/shard_map/all_gather | solution.py:31
  455.9 89.0 %reduce-scatter.15.cloned.1.call-start = ((), (), s32[]{:S(2)}) async-start(), calls=%async_computation.12 | async-start | bytes 2621440
  500.9 91.8 %all-gather.14.cloned.1.call-start = ((), (), s32[]{:S(2)}) async-start(), calls=%async_computation.7 | async-start | bytes 2621440 | tf_op jit(solution)/shard_map/all_gather | solution.py:42
  547.3 191.5 %all-reduce.9.cloned.1.call-start = ((), (), s32[]{:S(2)}) async-start(), calls=%async_computation.16 | async-start | bytes 4194304
  668.0 70.8 %slice-start.1 = ((f32[15,64,1024]{2,1,0:T(8,128)}), f32[2,64,1024]{2,1,0:T(8,128)S(1)}, s32[]{:S(2)}) async-start(f32[15,64,1024]{2,1,0:T(8,128)} %param.4), calls=%async_computation.19 | async-start | bytes 1048576 | tf_op jit(solution)/shard_map/slice | solution.py:22
  678.5 89.8 %all-gather.16.cloned.1.call-start = ((), (), s32[]{:S(2)}) async-start(), calls=%async_computation.8 | async-start | bytes 2359296 | tf_op jit(solution)/shard_map/all_gather | solution.py:31
  741.0 59.2 %reduce-scatter.17.cloned.1.call-start = ((), (), s32[]{:S(2)}) async-start(), calls=%async_computation.13 | async-start | bytes 1310720
  772.9 56.1 %all-gather.18.cloned.1.call-start = ((), (), s32[]{:S(2)}) async-start(), calls=%async_computation.9 | async-start | bytes 1310720 | tf_op jit(solution)/shard_map/all_gather | solution.py:42
  802.2 145.9 %all-reduce.11.cloned.1.call-start = ((), (), s32[]{:S(2)}) async-start(), calls=%async_computation.17 | async-start | bytes 4194304
  840.1 108.0 %slice-start.2 = ((f32[15,64,1024]{2,1,0:T(8,128)}), f32[1,64,1024]{2,1,0:T(8,128)S(1)}, s32[]{:S(2)}) async-start(f32[15,64,1024]{2,1,0:T(8,128)} %param.4), calls=%async_computation.20 | async-start | bytes 524288 | tf_op jit(solution)/shard_map/slice | solution.py:22
  887.0 86.0 %all-gather.20.cloned.1.call-start = ((), (), s32[]{:S(2)}) async-start(), calls=%async_computation.10 | async-start | bytes 1179648 | tf_op jit(solution)/shard_map/all_gather | solution.py:31
  950.2 47.7 %reduce-scatter.19.cloned.1.call-start = ((), (), s32[]{:S(2)}) async-start(), calls=%async_computation.14 | async-start | bytes 655360
Sparse Core Ops, SparseCore 0:
  9.4 57.0 all-gather.7
  85.3 76.7 reduce-scatter.12
  165.2 81.2 all-gather.9
  373.7 79.5 all-reduce.6
  456.0 36.7 all-gather.11
  501.0 43.8 reduce-scatter.14
  547.4 45.2 all-gather.13
  678.6 60.1 all-reduce.8
  741.2 27.0 all-gather.15
  773.1 27.1 reduce-scatter.16
  802.3 26.5 all-gather.17
  887.1 60.9 all-reduce.10
  950.3 22.6 all-gather.19
  976.3 21.5 reduce-scatter.18
where the time goes:
time: 1020 us; the launch traced here: 1010 us
  waiting for transfers between devices  667 us (65%)
  matrix products  267 us (26%)
  local copies, waits for them, and re-layouts  41.9 us (4%)
  other arithmetic  22.3 us (2%)
  between operations  14.3 us (1%)
    unnamed x21, waiting for transfers between devices  370 us
    dot_general x3, matrix products, per_device(): jnp.einsum('nst,nsci->cti', selector, products, precision=lax.Precision.H...  187 us
    all_gather x3, waiting for transfers between devices, per_device(): lax.all_gather(own_rows.astype(jnp.bfloat16), 'col', axis=0, tiled=True)  153 us
    all_gather x4, waiting for transfers between devices, per_device(): lax.all_gather(current.astype(jnp.bfloat16), 'row', axis=1, tiled=True)  144 us
    dot_general x3, matrix products, per_device(): jnp.einsum('cnk,nsik->nsci', solved_all, node_panels, preferred_element_t...  55.5 us
    dot_general x4, matrix products, per_device(): jnp.einsum('nck,nik->cni', gathered, inverse, preferred_element_type=jnp....  25.2 us
  transfers between devices with their start and end apart: 14, of which 14 were waited for; matrix products, arithmetic and copies ran while one was open for 0% of the time, Pallas kernels for 0%

commit v1 on v0

v1 whole, which is shorter than its diff:
```python
import functools

import jax
import jax.numpy as jnp
import numpy as np
from jax import lax
from jax.experimental import pallas as pl
from jax.experimental.pallas import tpu as pltpu
from jax.sharding import PartitionSpec as P

LEV = 4
S = 15
PARAMS = pltpu.CompilerParams(vmem_limit_bytes=32 * 2**20)
TRANSPOSED = (((1,), (1,)), ((), ()))


def first_of(level):
    return 2**LEV - 2 ** (level + 1)


def ancestor_table():
    table = np.full((S - 1, LEV - 1), -1, np.int32)
    for level in range(1, LEV):
        for j in range(2**level):
            for distance in range(1, level + 1):
                table[first_of(level) + j, distance - 1] = first_of(level - distance) + (j >> distance)
    return table


def inverse_kernel(residual_ref, inverse_ref, piece_ref):
    senders, _, share, depth = residual_ref.shape
    receivers, _, rows, width = piece_ref.shape
    x = residual_ref[...].reshape(senders * share, depth)
    product = lax.dot_general(x, inverse_ref[0], TRANSPOSED, preferred_element_type=jnp.float32)
    piece_ref[...] = product.astype(piece_ref.dtype).reshape(receivers, 1, rows, width)


def apply_inverse(gathered, inverse, level, receivers):
    senders, count, share, depth = gathered.shape
    width = inverse.shape[1]
    samples = senders * share
    first = first_of(level)
    return pl.pallas_call(
        inverse_kernel,
        grid=(count,),
        in_specs=[
            pl.BlockSpec((senders, 1, share, depth), lambda n: (0, n, 0, 0)),
            pl.BlockSpec((1, width, depth), lambda n: (first + n, 0, 0)),
        ],
        out_specs=pl.BlockSpec((receivers, 1, samples // receivers, width), lambda n: (0, n, 0, 0)),
        out_shape=jax.ShapeDtypeStruct((receivers, count, samples // receivers, width), jnp.bfloat16),
        compiler_params=PARAMS,
        cost_estimate=pl.CostEstimate(
            flops=2 * count * samples * depth * width,
            bytes_accessed=2 * count * (samples * depth + width * depth + samples * width),
            transcendentals=0,
        ),
        name="apply_inverse",
    )(gathered, inverse)


def update_kernel(node_of, slots_ref, solved_ref, panel_ref, *rest, has_initial):
    initial_ref = rest[0] if has_initial else None
    part_ref, total = rest[-2], rest[-1]
    a, d = pl.program_id(0), pl.program_id(1)

    @pl.when(d == 0)
    def _():
        total[...] = initial_ref[...].reshape(total.shape) if has_initial else jnp.zeros_like(total)

    @pl.when(slots_ref[node_of(a, d)] >= 0)
    def _():
        senders, _, rows, depth = solved_ref.shape
        x = solved_ref[...].reshape(senders * rows, depth)
        total[...] += lax.dot_general(x, panel_ref[0, 0], TRANSPOSED, preferred_element_type=jnp.float32)

    @pl.when(d == pl.num_programs(1) - 1)
    def _():
        part_ref[...] = total[...].astype(part_ref.dtype).reshape(part_ref.shape)


def add_update(solved, panels, slots, initial, level, target, receivers, dtype):
    senders, count, rows, depth = solved.shape
    width = panels.shape[2]
    samples = senders * rows
    targets = 2**target
    span = count // targets
    first = first_of(level)
    distance = level - target

    def node_of(a, d):
        return (first + a * span + d) * (LEV - 1) + distance - 1

    block = (receivers, 1, samples // receivers, width)
    total_spec = pl.BlockSpec(block, lambda a, d, slots: (0, a, 0, 0))
    in_specs = [
        pl.BlockSpec((senders, 1, rows, depth), lambda a, d, slots: (0, a * span + d, 0, 0)),
        pl.BlockSpec(
            (1, 1, width, depth),
            lambda a, d, slots: (first + a * span + d, jnp.maximum(slots[node_of(a, d)], 0), 0, 0),
        ),
    ]
    operands = [slots, solved, panels]
    if initial is not None:
        in_specs.append(total_spec)
        operands.append(initial)
    return pl.pallas_call(
        functools.partial(update_kernel, node_of, has_initial=initial is not None),
        grid_spec=pltpu.PrefetchScalarGridSpec(
            num_scalar_prefetch=1,
            grid=(targets, span),
            in_specs=in_specs,
            out_specs=total_spec,
            scratch_shapes=[pltpu.VMEM((samples, width), jnp.float32)],
        ),
        out_shape=jax.ShapeDtypeStruct((receivers, targets, samples // receivers, width), dtype),
        compiler_params=PARAMS,
        cost_estimate=pl.CostEstimate(
            flops=2 * count * samples * depth * width,
            bytes_accessed=2 * count * (samples * depth + width * depth) + 4 * targets * samples * width,
            transcendentals=0,
        ),
        name="add_update",
    )(*operands)


def per_device(right_sides, diag_inverse, panels, block_map):
    row_count = lax.axis_size("row")
    col_count = lax.axis_size("col")
    own_blocks = lax.dynamic_slice_in_dim(block_map, lax.axis_index("col"), 1, 1)[:, 0, :]
    named = own_blocks[:, None, :] == jnp.asarray(ancestor_table())[:, :, None]
    slot_ids = jnp.arange(own_blocks.shape[1], dtype=jnp.int32)
    slots = jnp.max(jnp.where(named, slot_ids, -1), axis=2).reshape(-1)
    pending = {}
    received = None
    results = []
    for level in range(LEV - 1, -1, -1):
        first, count = first_of(level), 2**level
        current = right_sides[first : first + count]
        if received is not None:
            current = current - jnp.sum(received.astype(jnp.float32), axis=0)
        gathered = lax.all_gather(current.astype(jnp.bfloat16), "row", axis=0)
        pieces = apply_inverse(gathered, diag_inverse, level, col_count)
        own = lax.psum_scatter(pieces, "col", scatter_dimension=0, tiled=False)
        results.append(own.astype(jnp.float32))
        if level > 0:
            solved = lax.all_gather(own, "col", axis=0)
            parts = add_update(
                solved, panels, slots, pending.get(level - 1), level, level - 1, row_count, jnp.bfloat16
            )
            received = lax.all_to_all(parts, "row", 0, 0, tiled=True)
            if level > 1:
                solved, received = lax.optimization_barrier((solved, received))
            for target in range(level - 2, -1, -1):
                pending[target] = add_update(
                    solved, panels, slots, pending.get(target), level, target, row_count, jnp.float32
                )
    return jnp.concatenate(results, axis=0)


def solution(mesh):
    return jax.shard_map(
        per_device,
        mesh=mesh,
        in_specs=(P(None, "row", "col"), P(None, "row", "col"), P(None, None, "col", "row"), P()),
        out_specs=P(None, "col", "row"),
        check_vma=False,
    )
```

time: 1020 us -> 666 us (0.65)
  matrix products: 267 us -> 0 us
  waiting for transfers between devices: 667 us -> 444 us
  blocking collectives: 0 us -> 101 us
  Pallas kernels: 0 us -> 51.6 us
  other arithmetic: 22.3 us -> 10.3 us
    unnamed x21 -> x11, waiting for transfers between devices: 370 us -> 0.18 us
    dot_general x10 -> x0, matrix products: 267 us -> none  [the longest x3 187 us: per_device(): jnp.einsum('nst,nsci->cti', selector, products, precision=lax.Precision.H...]
    reduce_scatter x0 -> x4, waiting for transfers between devices: none -> 170 us  [per_device(): own = lax.psum_scatter(pieces, 'col', scatter_dimension=0, tiled=False)]
    all_to_all x0 -> x3, blocking collectives: none -> 101 us  [per_device(): received = lax.all_to_all(parts, 'row', 0, 0, tiled=True)]
    pallas_call x0 -> x10, Pallas kernels: none -> 51.6 us  [the longest x6 34.1 us: add_update(): pl.pallas_call(functools.partial(update_kernel, node_of, has_initial=init...]
    unnamed x13 -> x45, local copies, waits for them, and re-layouts: 14.8 us -> 40.3 us
    all_gather x7, waiting for transfers between devices: 297 us -> 274 us  [the longest x4 143 us: per_device(): gathered = lax.all_gather(current.astype(jnp.bfloat16), 'row', axis=0)]
    slice x14 -> x1, local copies, waits for them, and re-layouts: 17.7 us -> 2.73 us  [per_device(): current = right_sides[first:first + count]]
  transfers between devices with their start and end apart: 14 -> 11, of which waited for: 14 -> 11; matrix products, arithmetic and copies ran while one was open for 0% -> 0% of each run, Pallas kernels for 0% -> 3%
where the time goes in v1:
time: 666 us; the launch traced here: 665 us
  waiting for transfers between devices  444 us (67%)
  blocking collectives  101 us (15%)
  Pallas kernels  51.6 us (8%)
  local copies, waits for them, and re-layouts  43.3 us (7%)
  between operations  13.4 us (2%)
  other arithmetic  10.3 us (2%)
    reduce_scatter x4, waiting for transfers between devices, per_device(): own = lax.psum_scatter(pieces, 'col', scatter_dimension=0, tiled=False)  170 us
    all_gather x4, waiting for transfers between devices, per_device(): gathered = lax.all_gather(current.astype(jnp.bfloat16), 'row', axis=0)  143 us
    all_gather x3, waiting for transfers between devices, per_device(): solved = lax.all_gather(own, 'col', axis=0)  131 us
    all_to_all x3, blocking collectives, per_device(): received = lax.all_to_all(parts, 'row', 0, 0, tiled=True)  101 us
    unnamed x45, local copies, waits for them, and re-layouts  40.3 us
    pallas_call x6, Pallas kernels, add_update(): pl.pallas_call(functools.partial(update_kernel, node_of, has_initial=init...  34.1 us
    pallas_call x4, Pallas kernels, apply_inverse(): pl.pallas_call(inverse_kernel, grid=(count,), in_specs=[pl.BlockSpec((sen...  17.5 us
  transfers between devices with their start and end apart: 11, of which 11 were waited for; matrix products, arithmetic and copies ran while one was open for 0% of the time, Pallas kernels for 3%

profile of v1, /device:TPU:0, one launch (start us, length us, event | category | flops | bytes accessed | tf_op | source)
XLA Modules:
  0.0 664.5 jit_solution(893232969516201467)
XLA Ops:
  6.5 2.7 slice.22
  9.3 57.2 %all-gather.18.cloned.1.call-done = bf16[64,64,1024]{2,1,0:T(8,128)(2,1)} async-done(((bf16[8,64,1024]{2,1,0:T(8,128)(2,1)}), bf16[64,64,1024]{2,1,0:T(8,128)(2,1)}) %all-gather.18.cloned.1.call-update) | async-done | bytes 8388624 | tf_op jit(solution)/shard_map/all_gather | solution.py:142
  66.5 3.4 copy-done.11
  69.9 9.3 %apply_inverse.4 = bf16[4,8,128,512]{3,2,1,0:T(8,128)(2,1)S(1)} custom-call(bf16[8,8,64,1024]{3,2,1,0:T(8,128)(2,1)S(1)} %bitcast.15, bf16[15,512,1024]{2,1,0:T(8,128)(2,1)} %inverse_ref.7), custom_call_target="tpu_custom_call" | custom-call | flops 4294967296 | bytes 20971520 | tf_op jit(solution)/shard_map/apply_inverse/pallas_call | solution.py:43
  79.3 2.0 copy-done.8
  81.3 76.9 %reduce-scatter.5.cloned.1.call-done = bf16[1,8,128,512]{3,2,1,0:T(8,128)(2,1)} async-done(((bf16[4,8,128,512]{3,2,1,0:T(8,128)(2,1)}), bf16[1,8,128,512]{3,2,1,0:T(8,128)(2,1)}) %reduce-scatter.5.cloned.1.call-update) | async-done | bytes 1048592 | tf_op jit(solution)/shard_map/reduce_scatter | solution.py:144
  158.3 0.1 copy.9
  158.5 82.6 %all-gather.12.cloned.1.call-done.solved_ref = bf16[4,8,128,512]{3,2,1,0:T(8,128)(2,1)} async-done(((bf16[1,8,128,512]{3,2,1,0:T(8,128)(2,1)}), bf16[4,8,128,512]{3,2,1,0:T(8,128)(2,1)}) %all-gather.12.cloned.1.call-update) | async-done | bytes 4194320 | tf_op jit(solution)/shard_map/all_gather | solution.py:147
  241.2 2.2 copy-done.5
  243.3 7.7 %add_update.6 = bf16[8,4,64,1024]{3,2,1,0:T(8,128)(2,1)S(1)} custom-call(s32[42]{0:T(128)S(1)} %reshape.25.slots_ref, bf16[4,8,128,512]{3,2,1,0:T(8,128)(2,1)S(1)} %copy-done.5, bf16[14,3,1024,512]{3,2,1,0:T(8,128)(2,1)} %panel_ref.11), custom_call_target="tpu_custom_call" | custom-call | flops 4294967296 | bytes 20971520 | tf_op jit(solution)/shard_map/add_update/pallas_call | solution.py:107
  251.0 52.6 %all_to_all.15 = bf16[8,4,64,1024]{3,2,1,0:T(8,128)(2,1)S(1)} all-to-all(bf16[8,4,64,1024]{3,2,1,0:T(8,128)(2,1)S(1)} %add_update.6), channel_id=1, replica_groups=mesh['row'=8,'col'=4] {'row'}, dimensions={0} | all-to-all | bytes 8388608 | tf_op jit(solution)/shard_map/all_to_all | solution.py:151
  303.6 0.9 convert_reduce_fusion
  304.5 2.2 subtract_convert_fusion
  306.7 36.3 %all-gather.20.cloned.1.call-done = bf16[32,64,1024]{2,1,0:T(8,128)(2,1)} async-done(((bf16[4,64,1024]{2,1,0:T(8,128)(2,1)}), bf16[32,64,1024]{2,1,0:T(8,128)(2,1)}) %all-gather.20.cloned.1.call-update) | async-done | bytes 4194320 | tf_op jit(solution)/shard_map/all_gather | solution.py:142
  343.1 5.5 copy-done.2
  348.5 2.2 copy-done.14
  350.7 4.1 apply_inverse.5
  354.9 44.0 %reduce-scatter.7.cloned.1.call-done = bf16[1,4,128,512]{3,2,1,0:T(8,128)(2,1)} async-done(((bf16[4,4,128,512]{3,2,1,0:T(8,128)(2,1)}), bf16[1,4,128,512]{3,2,1,0:T(8,128)(2,1)}) %reduce-scatter.7.cloned.1.call-update) | async-done | bytes 524304 | tf_op jit(solution)/shard_map/reduce_scatter | solution.py:144
  399.0 2.2 copy-done.6
  401.1 8.5 %add_update.7.rest_0_ = f32[8,2,64,1024]{3,2,1,0:T(8,128)S(1)} custom-call(s32[42]{0:T(128)S(1)} %reshape.25.slots_ref, bf16[4,8,128,512]{3,2,1,0:T(8,128)(2,1)S(1)} %copy-done.6, bf16[14,3,1024,512]{3,2,1,0:T(8,128)(2,1)} %panel_ref.11), custom_call_target="tpu_custom_call" | custom-call | flops 4294967296 | bytes 16777216 | tf_op jit(solution)/shard_map/add_update/pallas_call | solution.py:107
  409.6 2.0 copy-done.9
  411.6 34.0 %all-gather.14.cloned.1.call-done.solved_ref = bf16[4,4,128,512]{3,2,1,0:T(8,128)(2,1)} async-done(((bf16[1,4,128,512]{3,2,1,0:T(8,128)(2,1)}), bf16[4,4,128,512]{3,2,1,0:T(8,128)(2,1)}) %all-gather.14.cloned.1.call-update) | async-done | bytes 2097168 | tf_op jit(solution)/shard_map/all_gather | solution.py:147
  445.6 2.2 copy-done.10
  447.8 1.6 copy-done.12
  449.4 4.0 add_update.8
  453.4 30.1 %all_to_all.16 = bf16[8,2,64,1024]{3,2,1,0:T(8,128)(2,1)S(1)} all-to-all(bf16[8,2,64,1024]{3,2,1,0:T(8,128)(2,1)S(1)} %add_update.8), channel_id=1, replica_groups=mesh['row'=8,'col'=4] {'row'}, dimensions={0} | all-to-all | bytes 4194304 | tf_op jit(solution)/shard_map/all_to_all | solution.py:151
  483.4 0.4 convert_reduce_fusion.1
  483.8 1.8 subtract_convert_fusion.1
  485.7 27.1 %all-gather.22.cloned.1.call-done = bf16[16,64,1024]{2,1,0:T(8,128)(2,1)} async-done(((bf16[2,64,1024]{2,1,0:T(8,128)(2,1)}), bf16[16,64,1024]{2,1,0:T(8,128)(2,1)}) %all-gather.22.cloned.1.call-update) | async-done | bytes 2097168 | tf_op jit(solution)/shard_map/all_gather | solution.py:142
  512.8 5.5 copy-done.3
  518.2 1.6 copy-done.15
  519.8 2.5 apply_inverse.6
  522.4 27.2 %reduce-scatter.9.cloned.1.call-done = bf16[1,2,128,512]{3,2,1,0:T(8,128)(2,1)} async-done(((bf16[4,2,128,512]{3,2,1,0:T(8,128)(2,1)}), bf16[1,2,128,512]{3,2,1,0:T(8,128)(2,1)}) %reduce-scatter.9.cloned.1.call-update) | async-done | bytes 262160 | tf_op jit(solution)/shard_map/reduce_scatter | solution.py:144
  549.7 2.2 copy-done.7
  551.9 8.0 %add_update.9.rest_0_ = f32[8,1,64,1024]{3,2,1,0:T(8,128)S(1)} custom-call(s32[42]{0:T(128)S(1)} %reshape.25.slots_ref, bf16[4,8,128,512]{3,2,1,0:T(8,128)(2,1)S(1)} %copy-done.7, bf16[14,3,1024,512]{3,2,1,0:T(8,128)(2,1)} %panel_ref.11), custom_call_target="tpu_custom_call" | custom-call | flops 4294967296 | bytes 14680064 | tf_op jit(solution)/shard_map/add_update/pallas_call | solution.py:107
  559.8 3.8 add_update.10.rest_0_
  563.6 14.2 %all-gather.16.cloned.1.call-done.solved_ref = bf16[4,2,128,512]{3,2,1,0:T(8,128)(2,1)} async-done(((bf16[1,2,128,512]{3,2,1,0:T(8,128)(2,1)}), bf16[4,2,128,512]{3,2,1,0:T(8,128)(2,1)}) %all-gather.16.cloned.1.call-update) | async-done | bytes 1048592 | tf_op jit(solution)/shard_map/all_gather | solution.py:147
  577.9 1.2 copy-done.16
  579.1 2.3 add_update.11
  581.4 18.8 %all_to_all.17 = bf16[8,1,64,1024]{3,2,1,0:T(8,128)(2,1)S(1)} all-to-all(bf16[8,1,64,1024]{3,2,1,0:T(8,128)(2,1)S(1)} %add_update.11), channel_id=1, replica_groups=mesh['row'=8,'col'=4] {'row'}, dimensions={0} | all-to-all | bytes 2097152 | tf_op jit(solution)/shard_map/all_to_all | solution.py:151
  600.2 0.2 convert_reduce_fusion.2
  600.4 1.7 fusion
  602.1 22.6 %all-gather.24.cloned.1.call-done = bf16[8,64,1024]{2,1,0:T(8,128)(2,1)} async-done(((bf16[1,64,1024]{2,1,0:T(8,128)(2,1)}), bf16[8,64,1024]{2,1,0:T(8,128)(2,1)}) %all-gather.24.cloned.1.call-update) | async-done | bytes 1048592 | tf_op jit(solution)/shard_map/all_gather | solution.py:142
  624.7 5.5 copy-done.4
  630.2 1.2 copy-done.17
  631.4 1.5 apply_inverse.7
  633.0 21.8 %reduce-scatter.11.cloned.1.call-done = bf16[1,1,128,512]{3,2,1,0:T(8,128)(2,1)} async-done(((bf16[4,1,128,512]{3,2,1,0:T(8,128)(2,1)}), bf16[1,1,128,512]{3,2,1,0:T(8,128)(2,1)}) %reduce-scatter.11.cloned.1.call-update) | async-done | bytes 131088 | tf_op jit(solution)/shard_map/reduce_scatter | solution.py:144
  654.8 3.2 maximum_convert_fusion
  (55 shorter events, 0.8 us)
Async XLA Ops:
  6.5 151.7 %copy-start = (s32[14,4,3]{0,1,2:T(4,128)S(1)}, s32[14,4,3]{0,1,2:T(4,128)}, u32[]{:S(2)}) copy-start(s32[14,4,3]{0,1,2:T(4,128)} %param.8) | copy-start | bytes 2020
  6.5 60.0 %all-gather.18.cloned.1.call-start = ((), (), s32[]{:S(2)}) async-start(), calls=%async_computation.14 | async-start | bytes 9437184 | tf_op jit(solution)/shard_map/all_gather | solution.py:142
  9.3 148.9 %reduce-scatter.5.cloned.1.call-start = ((), (), s32[]{:S(2)}) async-start(), calls=%async_computation.7 | async-start | bytes 5242880 | tf_op jit(solution)/shard_map/reduce_scatter | solution.py:144
  66.5 3.4 copy-start.11
  79.3 2.0 copy-start.8
  81.2 77.1 %copy-start.21 = (s32[14,3]{0,1:T(4,128)S(1)}, s32[14,3]{0,1:T(4,128)}, u32[]{:S(2)}) copy-start(s32[14,3]{0,1:T(4,128)} %constant.16.clone) | copy-start | bytes 508
  81.3 159.9 %all-gather.12.cloned.1.call-start = ((), (), s32[]{:S(2)}) async-start(), calls=%async_computation.8 | async-start | bytes 5242880 | tf_op jit(solution)/shard_map/all_gather | solution.py:147
  158.2 184.9 %all-gather.20.cloned.1.call-start = ((), (), s32[]{:S(2)}) async-start(), calls=%async_computation.15 | async-start | bytes 4718592 | tf_op jit(solution)/shard_map/all_gather | solution.py:142
  241.1 2.2 copy-start.5
  306.7 92.2 %reduce-scatter.7.cloned.1.call-start = ((), (), s32[]{:S(2)}) async-start(), calls=%async_computation.9 | async-start | bytes 2621440 | tf_op jit(solution)/shard_map/reduce_scatter | solution.py:144
  343.1 5.5 copy-start.2
  348.5 2.2 copy-start.14
  354.9 90.7 %all-gather.14.cloned.1.call-start = ((), (), s32[]{:S(2)}) async-start(), calls=%async_computation.10 | async-start | bytes 2621440 | tf_op jit(solution)/shard_map/all_gather | solution.py:147
  398.9 113.8 %all-gather.22.cloned.1.call-start = ((), (), s32[]{:S(2)}) async-start(), calls=%async_computation.16 | async-start | bytes 2359296 | tf_op jit(solution)/shard_map/all_gather | solution.py:142
  399.0 2.2 copy-start.6
  409.6 2.0 copy-start.9
  445.6 2.2 copy-start.10
  447.8 1.6 copy-start.12
  485.6 64.0 %reduce-scatter.9.cloned.1.call-start = ((), (), s32[]{:S(2)}) async-start(), calls=%async_computation.11 | async-start | bytes 1310720 | tf_op jit(solution)/shard_map/reduce_scatter | solution.py:144
  512.7 5.5 copy-start.3
  518.2 1.6 copy-start.15
  522.3 55.6 %all-gather.16.cloned.1.call-start = ((), (), s32[]{:S(2)}) async-start(), calls=%async_computation.12 | async-start | bytes 1310720 | tf_op jit(solution)/shard_map/all_gather | solution.py:147
  549.6 75.1 %all-gather.24.cloned.1.call-start = ((), (), s32[]{:S(2)}) async-start(), calls=%async_computation.17 | async-start | bytes 1179648 | tf_op jit(solution)/shard_map/all_gather | solution.py:142
  549.7 2.2 copy-start.7
  551.9 8.0 %copy-start.13 = (bf16[4,4,128,512]{3,2,1,0:T(8,128)(2,1)S(1)}, bf16[4,4,128,512]{3,2,1,0:T(8,128)(2,1)}, u32[]{:S(2)}) copy-start(bf16[4,4,128,512]{3,2,1,0:T(8,128)(2,1)} %all-gather.14.cloned.1.call-done.solved_ref) | copy-start | bytes 6291460
  577.9 1.2 copy-start.16
  602.1 52.7 %reduce-scatter.11.cloned.1.call-start = ((), (), s32[]{:S(2)}) async-start(), calls=%async_computation.13 | async-start | bytes 655360 | tf_op jit(solution)/shard_map/reduce_scatter | solution.py:144
  624.7 5.5 copy-start.4
  630.2 1.2 copy-start.17
  631.4 23.4 %copy-start.18 = (bf16[1,8,128,512]{3,2,1,0:T(8,128)(2,1)S(1)}, bf16[1,8,128,512]{3,2,1,0:T(8,128)(2,1)}, u32[]{:S(2)}) copy-start(bf16[1,8,128,512]{3,2,1,0:T(8,128)(2,1)} %reduce-scatter.5.cloned.1.call-done) | copy-start | bytes 3145732
  631.4 23.4 %copy-start.19 = (bf16[1,4,128,512]{3,2,1,0:T(8,128)(2,1)S(1)}, bf16[1,4,128,512]{3,2,1,0:T(8,128)(2,1)}, u32[]{:S(2)}) copy-start(bf16[1,4,128,512]{3,2,1,0:T(8,128)(2,1)} %reduce-scatter.7.cloned.1.call-done) | copy-start | bytes 1572868
  631.4 23.4 %copy-start.20 = (bf16[1,2,128,512]{3,2,1,0:T(8,128)(2,1)S(1)}, bf16[1,2,128,512]{3,2,1,0:T(8,128)(2,1)}, u32[]{:S(2)}) copy-start(bf16[1,2,128,512]{3,2,1,0:T(8,128)(2,1)} %reduce-scatter.9.cloned.1.call-done) | copy-start | bytes 786436
  631.4 26.6 %copy-start.1 = (s32[14,4,3]{0,1,2:T(4,128)S(1)}, s32[14,4,3]{0,1,2:T(4,128)}, u32[]{:S(2)}) copy-start(s32[14,4,3]{0,1,2:T(4,128)} %param.8) | copy-start | bytes 2020
Sparse Core Ops, SparseCore 0:
  9.4 57.0 all-gather.17
  81.4 76.7 reduce-scatter.4
  159.8 81.2 all-gather.11
  306.8 36.1 all-gather.19
  355.0 43.8 reduce-scatter.6
  400.3 45.2 all-gather.13
  485.8 26.9 all-gather.21
  522.4 27.1 reduce-scatter.8
  551.3 26.5 all-gather.15
  602.2 22.4 all-gather.23
  633.1 21.6 reduce-scatter.10
